TPU v7x, 768 devices: a whole 4x8x12 slice. The times are simulated.
768 devices in a mesh: dp: 12 (over z), expert: 32 (over x, y), tensor: 2 (over core).
Axes of the slice: x: 4, y: 8, z: 12, core: 2. Of those that a mesh axis runs over, the one named last changes fastest.
Arguments:
- tokens: bfloat16 [49152, 3584], P(('dp', 'expert')), may hold values from -6 to 6
- routes: int32 [49152, 2], P(('dp', 'expert')), may hold values from 0 to 31, all different within a row; in each aligned block of 128 rows (0 to 127, 128 to 255, ...) at most 9 rows name the same one
- returns: float32 [49152], P(('dp', 'expert')), may hold values from -24 to 24
- router_weight: bfloat16 [3584, 32], replicated, may hold values from -0.09375 to 0.09375
- gate_weight: bfloat16 [32, 3584, 1024], P('expert', None, 'tensor'), may hold values from -0.09375 to 0.09375
- up_weight: bfloat16 [32, 3584, 1024], P('expert', None, 'tensor'), may hold values from -0.09375 to 0.09375
- down_weight: bfloat16 [32, 1024, 3584], P('expert', 'tensor'), may hold values from -0.1875 to 0.1875
- norm_gain: float32 [3584], replicated, may hold values from 0.1 to 1.9
- value_weight: bfloat16 [3584], replicated, may hold values from -0.09375 to 0.09375
Outputs:
- values: float32 [49152], P(('dp', 'expert'))
- router_grad: bfloat16 [3584, 32], replicated
Inputs may be any that keep to these rules, and one draw needn't show every extreme that they name: The 2 routes of a token are different experts. Among the tokens of one index of dp and expert no expert is named more than 9 times, and in every draw some such block names some expert exactly 9 times; every expert is named somewhere.
All inputs are finite; a program needn't handle non-finite values.
Results may differ from a plain program's by a relative error of at most 0.017.
Values may be sent and summed in bfloat16 or wider, within the bound.
A program may use at most 64 MiB of HBM per device.

v0:
```python
import jax
import jax.numpy as jnp
from jax import lax
from jax.sharding import PartitionSpec as P

eps = 1e-06
route_scale = 2.5


def rescale(raw):
    return jnp.sign(raw) * (jnp.sqrt(jnp.abs(raw) + 1.0) - 1.0) + 0.001 * raw


def head_and_router(
    tok_block, route_block, return_block, out_block, router_weight, norm_gain, value_weight
):
    logits = jnp.dot(tok_block, router_weight, preferred_element_type=jnp.float32)
    scores = jax.nn.sigmoid(logits)
    chosen = jnp.take_along_axis(scores, route_block, axis=1)
    score_sum = jnp.sum(chosen, axis=1, keepdims=True)
    weights = chosen / score_sum
    expert_f = out_block.astype(jnp.float32)
    mixture = jnp.einsum("tk,tkd->td", weights, expert_f)
    residual = tok_block.astype(jnp.float32) + route_scale * mixture
    inverse = lax.rsqrt(jnp.mean(residual * residual, axis=1, keepdims=True) + eps)
    gained = norm_gain * value_weight.astype(jnp.float32)
    values = jnp.sum(residual * inverse * gained[None, :], axis=1)
    value_error = values - rescale(return_block)
    direction = gained[None, :] * value_error[:, None]
    grad_resid = inverse * direction - residual * inverse * inverse * inverse * jnp.mean(
        residual * direction, axis=1, keepdims=True
    )
    grad_weights = route_scale * jnp.einsum("td,tkd->tk", grad_resid, expert_f)
    centered = grad_weights - jnp.sum(weights * grad_weights, axis=1, keepdims=True)
    grad_logits = centered / score_sum * chosen * (1.0 - chosen)
    columns = jnp.arange(router_weight.shape[1], dtype=jnp.int32)
    marks = (route_block[:, :, None] == columns[None, None, :]).astype(jnp.float32)
    dense_grad = jnp.sum(marks * grad_logits[:, :, None], axis=1).astype(jnp.bfloat16)
    return (values, dense_grad)


def on_device(
    tokens,
    routes,
    returns,
    router_weight,
    gate_weight,
    up_weight,
    down_weight,
    norm_gain,
    value_weight,
):
    tok_count, model_width = tokens.shape
    per_token = routes.shape[1]
    groups = lax.axis_size("expert")
    capacity = max(2, (9 * tok_count * per_token + 8 * groups - 1) // (8 * groups))
    flat_routes = routes.reshape(-1)
    onehot = (flat_routes[:, None] == jnp.arange(groups, dtype=jnp.int32)[None, :]).astype(
        jnp.int32
    )
    position = jnp.sum(jnp.cumsum(onehot, axis=0) * onehot, axis=1) - 1
    slot_index = position * groups + flat_routes
    outgoing = jnp.zeros((capacity * groups, model_width), jnp.bfloat16)
    outgoing = outgoing.at[slot_index].set(jnp.repeat(tokens, per_token, axis=0))
    outgoing = outgoing.reshape(capacity, groups, model_width)
    gate_local = gate_weight[0]
    up_local = up_weight[0]
    down_local = down_weight[0]
    arrived_rows = lax.all_to_all(outgoing, "expert", split_axis=1, concat_axis=1, tiled=True)
    arrived = arrived_rows.shape[0]
    stacked = arrived_rows.reshape(-1, model_width)
    gate = jnp.dot(stacked, gate_local, preferred_element_type=jnp.float32)
    upward = jnp.dot(stacked, up_local, preferred_element_type=jnp.float32)
    hidden = (jax.nn.silu(gate) * upward).astype(jnp.bfloat16)
    partial_value = jnp.dot(hidden, down_local, preferred_element_type=jnp.float32)
    summed = lax.psum(partial_value.astype(jnp.bfloat16), "tensor")
    answer = lax.all_to_all(
        summed.reshape(arrived, groups, model_width),
        "expert",
        split_axis=1,
        concat_axis=1,
        tiled=True,
    )
    expert_out = answer.reshape(capacity * groups, model_width)[slot_index]
    expert_out = expert_out.reshape(tok_count, per_token, model_width)
    values, dense_grad = head_and_router(
        tokens, routes, returns, expert_out, router_weight, norm_gain, value_weight
    )
    term = lax.dot_general(
        tokens, dense_grad, (((0,), (0,)), ((), ())), preferred_element_type=jnp.float32
    )
    router_grad = lax.psum(term, ("dp", "expert")).astype(jnp.bfloat16)
    return (values, router_grad)


def solution(mesh):
    return jax.shard_map(
        on_device,
        mesh=mesh,
        in_specs=(
            P(("dp", "expert"), None),
            P(("dp", "expert"), None),
            P(("dp", "expert")),
            P(),
            P("expert", None, "tensor"),
            P("expert", None, "tensor"),
            P("expert", "tensor", None),
            P(),
            P(),
        ),
        out_specs=(P(("dp", "expert")), P()),
        check_vma=False,
    )
```

profile of v0, /device:TPU:512, one launch (start us, length us, event | category | flops | bytes accessed | tf_op | source)
XLA Modules:
  0.0 2339.1 jit_solution(1508764502932508390)
XLA Ops:
  7.2 0.0 copy-start
  7.2 0.0 all-reduce.3.cloned.1.call-start
  7.2 0.8 copy.65
  8.1 0.1 eq.42
  8.2 0.1 eq.38
  8.3 0.1 reshape.104
  8.5 0.6 reduce-window.6
  9.1 0.2 slice_reduce_fusion
  9.3 0.1 fusion.31
  9.4 2.1 broadcast_in_dim.10
  11.6 1.7 reshape.129
  13.3 4.7 scatter_custom_fusion
  17.9 1.3 copy.69
  19.2 94.0 %all_to_all.10 = bf16[9,32,3584]{2,0,1:T(8,128)(2,1)S(1)} all-to-all(bf16[9,32,3584]{2,0,1:T(8,128)(2,1)S(1)} %copy.69), channel_id=1, replica_groups=mesh['dp'=12,'expert'=32,'tensor'=2] {'expert'}, dimensions={1} | all-to-all | bytes 4128768 | tf_op jit(solution)/shard_map/all_to_all | solution.py:69
  113.2 1.3 copy.70
  114.5 0.8 copy-done.6
  115.3 1.2 fusion.3
  116.5 6.9 convolution_convert_fusion
  123.4 4.7 copy.71
  128.1 0.0 all-reduce.3.cloned.1.call-update
  128.1 0.0 copy-start.2
  128.1 0.0 copy-start.1
  128.2 42.8 %all-reduce.3.cloned.1.call-done = bf16[9,32,3584]{2,0,1:T(8,128)(2,1)} async-done(((bf16[9,32,3584]{2,0,1:T(8,128)(2,1)}), bf16[9,32,3584]{2,0,1:T(8,128)(2,1)}) %all-reduce.3.cloned.1.call-update) | async-done | bytes 2064400 | tf_op jit(solution)/shard_map/psum | solution.py:76
  171.0 9.9 all-to-all-start.1
  180.9 0.1 copy.63
  181.0 0.1 reshape.119
  181.2 0.4 fusion.19
  181.6 0.0 copy-start.3
  181.6 0.0 copy-start.4
  181.6 2.0 gather_fusion.1
  183.6 0.1 reshape.122
  183.7 0.1 copy.64
  183.8 0.2 copy.73
  184.1 82.8 %all-to-all-done.1 = bf16[9,32,3584]{2,0,1:T(8,128)(2,1)} async-done(((bf16[9,32,3584]{2,0,1:T(8,128)(2,1)}), bf16[9,32,3584]{2,0,1:T(8,128)(2,1)}, u32[]{:S(2)}, u32[]{:S(2)}) %all-to-all-start.1) | async-done | bytes 2064416 | tf_op jit(solution)/shard_map/all_to_all | solution.py:77
  266.8 3.3 copy.72
  270.1 3.0 gather_fusion
  273.1 3.9 reshape.110
  277.0 2.0 fusion.37
  279.1 0.4 multiply_reduce_fusion.1
  279.4 0.0 copy-start.7
  279.5 0.5 multiply_reduce_fusion
  279.9 0.2 copy-done.7
  280.1 0.5 fusion.7
  280.6 0.8 fusion.6
  281.4 4.1 fusion.9
  285.5 0.1 copy.76
  285.7 0.3 convolution_bitcast_fusion
  285.9 2046.3 %all-reduce.4 = bf16[3584,32]{0,1:T(8,128)(2,1)} all-reduce(f32[3584,32]{0,1:T(8,128)S(1)} %convolution_bitcast_fusion), channel_id=1, replica_groups=mesh['dp'=12,'expert'=32,'tensor'=2] {'dp','expert'}, use_global_device_ids=true, to_apply=%region_11.12 | all-reduce | flops 114688 | bytes 688128 | tf_op jit(solution)/shard_map/psum | solution.py:92
  (24 shorter events, 0.2 us)
Async XLA Ops:
  7.2 174.0 %copy-start = (bf16[3584,32]{0,1:T(8,128)(2,1)S(1)}, bf16[3584,32]{0,1:T(8,128)(2,1)}, u32[]{:S(2)}) copy-start(bf16[3584,32]{0,1:T(8,128)(2,1)} %param.12) | copy-start | bytes 688132
  7.2 163.8 %all-reduce.3.cloned.1.call-start = ((), (), s32[]{:S(2)}) async-start(), calls=%async_computation.2 | async-start | bytes 7340032 | tf_op jit(solution)/shard_map/psum | solution.py:76
  113.2 2.0 copy-start.6
  128.1 52.8 %copy-start.2 = (s32[128,2]{0,1:T(2,128)S(1)}, s32[128,2]{0,1:T(2,128)}, u32[]{:S(2)}) copy-start(s32[128,2]{0,1:T(2,128)} %param.10) | copy-start | bytes 3076
  128.1 53.0 %copy-start.1 = (bf16[128,3584]{1,0:T(8,128)(2,1)S(1)}, bf16[128,3584]{1,0:T(8,128)(2,1)}, u32[]{:S(2)}) copy-start(bf16[128,3584]{1,0:T(8,128)(2,1)} %param.9) | copy-start | bytes 2752516
  171.0 95.8 %all-to-all-start.1 = ((bf16[9,32,3584]{2,0,1:T(8,128)(2,1)}), bf16[9,32,3584]{2,0,1:T(8,128)(2,1)}, u32[]{:S(2)}, u32[]{:S(2)}) async-start(bf16[9,32,3584]{2,0,1:T(8,128)(2,1)} %all-reduce.3.cloned.1.call-done), calls=%async_computation.1 | async-start | bytes 7340032 | tf_op jit(solution)/shard_map/all_to_all | solution.py:77
  181.6 2.4 copy-start.3
  181.6 2.4 copy-start.4
  279.4 0.7 copy-start.7
  280.1 1.2 copy-start.5
Sparse Core Ops, SparseCore 0:
  128.3 42.6 all-reduce.2
where the time goes:
time: 2340 us
  blocking collectives  2140 us (91%)
  waiting for transfers between devices  126 us (5%)
  local copies, waits for them, and re-layouts  30.9 us (1%)
    psum x1, blocking collectives, on_device(): router_grad = lax.psum(term, ('dp', 'expert')).astype(jnp.bfloat16)  2050 us
    all_to_all x1, blocking collectives, on_device(): lax.all_to_all(outgoing, 'expert', split_axis=1, concat_axis=1, tiled=True)  94 us
    all_to_all x1, waiting for transfers between devices, on_device(): lax.all_to_all(summed.reshape(arrived, groups, model_width), 'expert', sp...  82.8 us
  transfers between devices with their start and end apart: 2, of which 2 were waited for; matrix products, arithmetic and copies ran while one was open for 0% of the time, Pallas kernels for 0%

commit v1 on v0

v1 whole, which is shorter than its diff:
```python
import functools
import jax
import jax.numpy as jnp
from jax import lax
from jax.experimental import pallas as pl
from jax.experimental.pallas import tpu as pltpu
from jax.sharding import PartitionSpec as P

MESH = pl.DeviceIdType.MESH
F32 = jnp.float32
BF16 = jnp.bfloat16
eps = 1e-06
route_scale = 2.5
LANES = 128
EIGHT = 8
TILE = 16


class Plan:
    def __init__(self, mesh, tokens, width, hidden):
        self.nz, self.groups = mesh.shape["dp"], mesh.shape["expert"]
        self.ny = 8 if self.groups >= 32 else 2
        self.nx = self.groups // self.ny
        self.steps = ((0, 4), (3, 5), (2, 6), (1, 7)) if self.ny == 8 else ((0,), (1,))
        self.chunks = len(self.steps)
        self.each = self.groups // self.chunks
        self.tokens, self.width, self.hidden = tokens, width, hidden
        self.half = width // 2
        self.quarter = width // 4
        self.pieces = self.half // LANES
        self.packed = self.quarter + LANES
        self.main = self.each * EIGHT
        self.rows = self.main + max(TILE, self.each)


def expert_kernel(
    plan,
    tok_ref,
    routes_ref,
    returns_ref,
    router_ref,
    gate_hbm,
    up_hbm,
    down_hbm,
    gain_ref,
    head_ref,
    values_ref,
    grad_ref,
    wg,
    wu,
    wd,
    out,
    arr,
    oth,
    xs,
    pxo,
    pxi,
    ret,
    back,
    qs,
    mix,
    nine,
    tmp9,
    wide9,
    chosen_ref,
    sums_out,
    sums_in,
    dlo,
    dli,
    zb,
    row9,
    agb,
    w_sem,
    out_s,
    out_r,
    fwd_s,
    fwd_r,
    px_s,
    px_r,
    ret_s,
    ret_r,
    sum_s,
    sum_r,
    dl_s,
    dl_r,
    z_s,
    z_r,
    ag_s,
    ag_r,
    agx_s,
    agx_r,
):
    T, D, H, Q4 = plan.tokens, plan.width, plan.half, plan.quarter
    NZ, NE, NX, NY = plan.nz, plan.groups, plan.nx, plan.ny
    NC, CD, MAIN, XR = plan.chunks, plan.each, plan.main, plan.rows
    z = lax.axis_index("dp")
    me = lax.axis_index("expert")
    c = lax.axis_index("tensor")
    other = 1 - c
    mx, my = lax.div(me, NY), lax.rem(me, NY)

    def hops(j, i):
        dx, b = lax.rem(i, NX), lax.div(i, NX)
        first = plan.steps[j][0]
        return dx, (first + b * (plan.steps[j][1] - first) if len(plan.steps[j]) > 1 else first)

    def ahead(j, i):
        dx, dy = hops(j, i)
        return lax.rem(mx + dx, NX) * NY + lax.rem(my + dy, NY)

    def behind(j, i):
        dx, dy = hops(j, i)
        return lax.rem(mx - dx + NX, NX) * NY + lax.rem(my - dy + NY, NY)

    def partners(j, body):
        def run(i, carry):
            body(jnp.int32(j * CD) + i, i)
            return carry

        lax.fori_loop(1 if j == 0 else 0, CD, run, 0)

    loads = [
        pltpu.make_async_copy(gate_hbm.at[0], wg, w_sem.at[0]),
        pltpu.make_async_copy(up_hbm.at[0], wu, w_sem.at[1]),
        pltpu.make_async_copy(down_hbm.at[0, :, pl.ds(0, H)], wd.at[0], w_sem.at[2]),
        pltpu.make_async_copy(down_hbm.at[0, :, pl.ds(H, H)], wd.at[1], w_sem.at[3]),
    ]
    for load in loads:
        load.start()

    barrier = pltpu.get_barrier_semaphore()
    for j in range(NC):
        partners(
            j,
            lambda d, i, j=j: pl.semaphore_signal(
                barrier, inc=1, device_id=(z, ahead(j, i), c), device_id_type=MESH
            ),
        )

    def greet(dz, carry):
        pl.semaphore_signal(
            barrier, inc=1, device_id=(lax.rem(z + dz, NZ), me, c), device_id_type=MESH
        )
        return carry

    lax.fori_loop(1, NZ, greet, 0)
    pl.semaphore_signal(barrier, inc=1, device_id=(z, me, other), device_id_type=MESH)

    def out_copy(j, d, i):
        return pltpu.make_async_remote_copy(
            out.at[d], arr.at[d], out_s.at[d], out_r.at[d], (z, ahead(j, i), c), MESH
        )

    def fwd_copy(d):
        return pltpu.make_async_remote_copy(
            arr.at[d], oth.at[d], fwd_s.at[d], fwd_r.at[d], (z, me, other), MESH
        )

    def px_copy(j):
        part = pl.ds(j * CD, CD)
        return pltpu.make_async_remote_copy(
            pxo.at[part], pxi.at[part], px_s.at[j], px_r.at[j], (z, me, other), MESH
        )

    def ret_copy(j, d, i):
        return pltpu.make_async_remote_copy(
            ret.at[d], back.at[d], ret_s.at[d], ret_r.at[d], (z, behind(j, i), c), MESH
        )

    def dl_copy(j, d, i):
        return pltpu.make_async_remote_copy(
            dlo.at[j], dli.at[d], dl_s.at[d], dl_r.at[d], (z, ahead(j, i), c), MESH
        )

    lane = lax.broadcasted_iota(jnp.int32, (1, LANES), 1)
    lane_i = jnp.where(lane < MAIN, lax.shift_right_logical(lane, 3), lane - MAIN)
    lane_slot = jnp.where(lane < MAIN, jnp.bitwise_and(lane, 7) + 1, EIGHT + 1)
    lane_slot = jnp.where(lane < MAIN + CD, lane_slot, -1).astype(F32)
    x_bits = NX.bit_length() - 1
    lane_dx = jnp.bitwise_and(lane_i, NX - 1)
    lane_b = lax.shift_right_logical(lane_i, x_bits)

    def lane_expert(j):
        dy = jnp.full((1, LANES), plan.steps[j][0], jnp.int32)
        for b in range(1, len(plan.steps[j])):
            dy = jnp.where(lane_b == b, plan.steps[j][b], dy)
        ex = jnp.bitwise_and(mx + lane_dx, NX - 1)
        ey = jnp.bitwise_and(my + dy, NY - 1)
        return ex * NY + ey

    def pack(dst, j, rows):
        part = pl.ds(j * CD, CD)
        first = rows[0:MAIN, 0:Q4].reshape(CD, EIGHT, Q4)
        second = rows[0:MAIN, Q4:H].reshape(CD, EIGHT, Q4)
        dst[part, :, 0:Q4] = jnp.concatenate([first, second], axis=1).astype(BF16)
        for q in range(plan.pieces):
            nine[pl.ds(q, CD, stride=TILE), :] = rows[MAIN : MAIN + CD, q * LANES : (q + 1) * LANES]
        dst[part, :, Q4:] = nine[...].reshape(CD, TILE, LANES).astype(BF16)

    def unpack(src, j, put):
        part = pl.ds(j * CD, CD)
        both = src[part, :, 0:Q4].astype(F32)
        put(0, MAIN, 0, Q4, both[:, 0:EIGHT].reshape(MAIN, Q4).astype(BF16))
        put(0, MAIN, Q4, Q4, both[:, EIGHT:TILE].reshape(MAIN, Q4).astype(BF16))
        tmp9[...] = src[part, :, Q4:].astype(F32).reshape(CD * TILE, LANES)
        last = jnp.concatenate(
            [tmp9[pl.ds(q, CD, stride=TILE), :] for q in range(plan.pieces)], axis=1
        )
        last = jnp.concatenate([last, jnp.zeros((XR - MAIN - CD, H), F32)], axis=0)
        put(MAIN, XR - MAIN, 0, H, last.astype(BF16))

    expert_of_row = lax.broadcasted_iota(jnp.int32, (LANES, T), 0)
    marks = [
        jnp.transpose((expert_of_row == routes_ref[k : k + 1, :]).astype(F32)) for k in range(2)
    ]
    earlier = (
        lax.broadcasted_iota(jnp.int32, (T, T), 0) > lax.broadcasted_iota(jnp.int32, (T, T), 1)
    ).astype(BF16)
    cum = jnp.dot(earlier, (marks[0] + marks[1]).astype(BF16), preferred_element_type=F32)
    key = jnp.concatenate([marks[0] * (cum + 1.0), marks[1] * (cum + 1.0)], axis=0).astype(BF16)
    nine[...] = jnp.zeros_like(nine)

    columns = pl.ds(pl.multiple_of(c * H, LANES), H)
    for j in range(NC):
        spread = (
            lax.broadcasted_iota(jnp.int32, (LANES, LANES), 0) == lane_expert(j)
        ).astype(BF16)
        named = jnp.dot(key, spread, preferred_element_type=F32)
        place = (named == lane_slot).astype(F32)
        qs[j] = place.astype(BF16)
        pick = jnp.transpose(place[0:T] + place[T : 2 * T])[0:XR].astype(BF16)
        rows = jnp.dot(pick, tok_ref[:, columns], preferred_element_type=F32)
        pack(out, j, rows)
        if j == 0:
            pl.semaphore_wait(barrier, NE - 1 + NZ - 1 + 1)
            arr[0] = out[0]
            fwd_copy(0).start()
        partners(j, lambda d, i, j=j: out_copy(j, d, i).start())

    logits = lax.dot_general(
        tok_ref[...], router_ref[...], (((1,), (1,)), ((), ())), preferred_element_type=F32
    )
    scores = jax.nn.sigmoid(logits)
    for k in range(2):
        chosen = jnp.sum(marks[k][:, 0:NE] * scores, axis=1, keepdims=True)
        chosen_ref[k] = jnp.broadcast_to(chosen, (T, LANES))

    for load in loads:
        load.wait()

    for j in range(NC):

        def arrive(d, i, j=j):
            out_copy(j, d, i).wait_recv()
            fwd_copy(d).start()

        partners(j, arrive)

        def put_own(r, n, col, m, v, j=j):
            xs[j, c, r : r + n, col : col + m] = v

        def put_other(r, n, col, m, v, j=j):
            xs[j, other, r : r + n, col : col + m] = v

        unpack(arr, j, put_own)

        def forwarded(i, carry, j=j):
            fwd_copy(jnp.int32(j * CD) + i).wait_recv()
            return carry

        lax.fori_loop(0, CD, forwarded, 0)
        unpack(oth, j, put_other)
        gate = jnp.dot(xs[j, 0], wg[0:H, :], preferred_element_type=F32)
        gate = gate + jnp.dot(xs[j, 1], wg[H:D, :], preferred_element_type=F32)
        upward = jnp.dot(xs[j, 0], wu[0:H, :], preferred_element_type=F32)
        upward = upward + jnp.dot(xs[j, 1], wu[H:D, :], preferred_element_type=F32)
        hidden = (gate / (1.0 + jnp.exp(-gate)) * upward).astype(BF16)
        pack(pxo, j, jnp.dot(hidden, wd[other], preferred_element_type=F32))
        px_copy(j).start()
        pack(ret, j, jnp.dot(hidden, wd[c], preferred_element_type=F32))
        px_copy(j).wait_recv()
        part = pl.ds(j * CD, CD)
        ret[part] = (ret[part].astype(F32) + pxi[part].astype(F32)).astype(BF16)
        if j == 0:
            back[0] = ret[0]
        partners(j, lambda d, i, j=j: ret_copy(j, d, i).start())

    for j in range(NC):
        partners(j, lambda d, i, j=j: ret_copy(j, d, i).wait_recv())

        pieces = {}

        def keep(r, n, col, m, v, pieces=pieces):
            pieces[(r, col)] = v

        unpack(back, j, keep)
        low = qs[j][:, 0:MAIN]
        high = qs[j][:, MAIN:XR]
        for col in (0, Q4):
            term = jnp.dot(low, pieces[(0, col)], preferred_element_type=F32)
            term = term + jnp.dot(
                high, pieces[(MAIN, 0)][:, col : col + Q4], preferred_element_type=F32
            )
            if j == 0:
                mix[:, col : col + Q4] = term
            else:
                mix[:, col : col + Q4] += term

    block = min(32, T)
    for b in range(T // block):
        low, high = b * block, (b + 1) * block
        first, second = chosen_ref[0, low:high], chosen_ref[1, low:high]
        total = first + second
        w0, w1 = first / total, second / total
        acc = [jnp.zeros((block, LANES), F32) for _ in range(6)]
        for q in range(plan.pieces):
            at = pl.ds(pl.multiple_of(c * H + q * LANES, LANES), LANES)
            gained = gain_ref[:, at] * head_ref[:, at].astype(F32)
            o0 = mix[low:high, q * LANES : (q + 1) * LANES]
            o1 = mix[T + low : T + high, q * LANES : (q + 1) * LANES]
            residual = tok_ref[low:high, at].astype(F32) + route_scale * (w0 * o0 + w1 * o1)
            terms = (
                residual * residual,
                residual * gained,
                residual * o0,
                residual * o1,
                gained * o0,
                gained * o1,
            )
            acc = [a + term for a, term in zip(acc, terms)]
        line = jnp.zeros((block, LANES), F32)
        for n, a in enumerate(acc):
            line = jnp.where(lane == n, jnp.sum(a, axis=1, keepdims=True), line)
        sums_out[low:high, :] = line

    sums_copy = pltpu.make_async_remote_copy(
        sums_out, sums_in, sum_s, sum_r, (z, me, other), MESH
    )
    sums_copy.start()
    raw = jnp.transpose(jnp.broadcast_to(returns_ref[...], (LANES, T)))[:, 0:1]
    sign = jnp.where(raw > 0.0, 1.0, jnp.where(raw < 0.0, -1.0, 0.0))
    target = sign * (jnp.sqrt(jnp.abs(raw) + 1.0) - 1.0) + 0.001 * raw
    first, second = chosen_ref[0][:, 0:1], chosen_ref[1][:, 0:1]
    score_sum = first + second
    w0, w1 = first / score_sum, second / score_sum
    sums_copy.wait_recv()
    sums = sums_out[...] + sums_in[...]
    rr, rg, ro0, ro1, go0, go1 = [sums[:, n : n + 1] for n in range(6)]
    inverse = lax.rsqrt(rr * (1.0 / D) + eps)
    values = rg * inverse
    values_ref[...] = jnp.transpose(jnp.broadcast_to(values, (T, LANES)))[0:1, :]
    error = values - target
    pull = inverse * inverse * inverse * (error * rg * (1.0 / D))
    gw0 = route_scale * (inverse * error * go0 - pull * ro0)
    gw1 = route_scale * (inverse * error * go1 - pull * ro1)
    centre = w0 * gw0 + w1 * gw1
    gl0 = (gw0 - centre) / score_sum * first * (1.0 - first)
    gl1 = (gw1 - centre) / score_sum * second * (1.0 - second)
    both = jnp.concatenate([gl0, gl1], axis=0).astype(BF16).astype(F32)

    for j in range(NC):
        dlo[j] = jnp.sum(qs[j].astype(F32) * both, axis=0, keepdims=True)
        if j == 0:
            dli[0] = dlo[0]
        partners(j, lambda d, i, j=j: dl_copy(j, d, i).start())

    grad = jnp.zeros((1, H), F32)
    for j in range(NC):
        partners(j, lambda d, i, j=j: dl_copy(j, d, i).wait_recv())
        got = dli[j * CD : (j + 1) * CD]
        mine = lax.broadcasted_iota(jnp.int32, (CD, 1, LANES), 0) == lane_i.reshape(1, 1, LANES)
        line = jnp.sum(jnp.where(mine, got, 0.0), axis=0)
        line = jnp.broadcast_to(line, (TILE, LANES)).astype(BF16)[:, 0:XR]
        grad = grad + jnp.dot(line, xs[j, c], preferred_element_type=F32)[0:1]

    zb[z] = grad

    def z_copy(dz):
        return pltpu.make_async_remote_copy(
            zb.at[z], zb.at[z], z_s.at[dz], z_r.at[z], (lax.rem(z + dz, NZ), me, c), MESH
        )

    def z_from(dz):
        source = lax.rem(z - dz + NZ, NZ)
        return pltpu.make_async_remote_copy(
            zb.at[source], zb.at[source], z_s.at[dz], z_r.at[source], (source, me, c), MESH
        )

    def z_start(dz, carry):
        z_copy(dz).start()
        return carry

    def z_wait(dz, carry):
        z_from(dz).wait_recv()
        return carry

    lax.fori_loop(1, NZ, z_start, 0)
    lax.fori_loop(1, NZ, z_wait, 0)
    grad = zb[0]
    for source in range(1, NZ):
        grad = grad + zb[source]

    row9[...] = jnp.zeros_like(row9)
    for q in range(plan.pieces):
        row9[q : q + 1, :] = grad[:, q * LANES : (q + 1) * LANES]
    agb[c, me] = row9[...].astype(BF16)

    def ag_copy(j, d, i):
        return pltpu.make_async_remote_copy(
            agb.at[c, me], agb.at[c, me], ag_s.at[d], ag_r.at[d], (z, ahead(j, i), c), MESH
        )

    def ag_from(j, d, i):
        source = behind(j, i)
        return pltpu.make_async_remote_copy(
            agb.at[c, source], agb.at[c, source], ag_s.at[d], ag_r.at[d], (z, source, c), MESH
        )

    for j in range(NC):
        partners(j, lambda d, i, j=j: ag_copy(j, d, i).start())
    for j in range(NC):
        partners(j, lambda d, i, j=j: ag_from(j, d, i).wait_recv())
    agx = pltpu.make_async_remote_copy(
        agb.at[c], agb.at[c], agx_s, agx_r, (z, me, other), MESH
    )
    agx.start()

    for j in range(NC):
        px_copy(j).wait_send()

        def left(d, i, j=j):
            out_copy(j, d, i).wait_send()
            ret_copy(j, d, i).wait_send()
            dl_copy(j, d, i).wait_send()
            ag_copy(j, d, i).wait_send()

        partners(j, left)

    def left_chip(d, carry):
        fwd_copy(d).wait_send()
        return carry

    def left_plane(dz, carry):
        z_copy(dz).wait_send()
        return carry

    lax.fori_loop(0, NE, left_chip, 0)
    lax.fori_loop(1, NZ, left_plane, 0)
    sums_copy.wait_send()

    def write(part):
        wide9[...] = agb[part].astype(F32).reshape(NE * TILE, LANES)
        for q in range(plan.pieces):
            at = pl.ds(pl.multiple_of(part * H + q * LANES, LANES), LANES)
            grad_ref[:, at] = wide9[pl.ds(q, NE, stride=TILE), :].astype(BF16)

    write(c)
    agx.wait()
    write(other)


def on_device(
    mesh,
    tokens,
    routes,
    returns,
    router_weight,
    gate_weight,
    up_weight,
    down_weight,
    norm_gain,
    value_weight,
):
    count, width = tokens.shape
    hidden = gate_weight.shape[2]
    plan = Plan(mesh, count, width, hidden)
    NE, NC, H = plan.groups, plan.chunks, plan.half
    packed = (NE, TILE, plan.packed)
    vmem, dma = pltpu.VMEM, pltpu.SemaphoreType.DMA
    in_vmem = pl.BlockSpec(memory_space=pltpu.VMEM)
    in_place = pl.BlockSpec(memory_space=pl.ANY)
    values, grad = pl.pallas_call(
        functools.partial(expert_kernel, plan),
        out_shape=(
            jax.ShapeDtypeStruct((1, count), F32),
            jax.ShapeDtypeStruct((NE, width), BF16),
        ),
        in_specs=[in_vmem] * 4 + [in_place] * 3 + [in_vmem] * 2,
        out_specs=(in_vmem, in_vmem),
        scratch_shapes=[
            vmem((width, hidden), BF16),
            vmem((width, hidden), BF16),
            vmem((2, hidden, H), BF16),
            vmem(packed, BF16),
            vmem(packed, BF16),
            vmem(packed, BF16),
            vmem((NC, 2, plan.rows, H), BF16),
            vmem(packed, BF16),
            vmem(packed, BF16),
            vmem(packed, BF16),
            vmem(packed, BF16),
            vmem((NC, 2 * count, LANES), BF16),
            vmem((2 * count, H), F32),
            vmem((plan.each * TILE, LANES), F32),
            vmem((plan.each * TILE, LANES), F32),
            vmem((NE * TILE, LANES), F32),
            vmem((2, count, LANES), F32),
            vmem((count, LANES), F32),
            vmem((count, LANES), F32),
            vmem((NC, 1, LANES), F32),
            vmem((NE, 1, LANES), F32),
            vmem((plan.nz, 1, H), F32),
            vmem((TILE, LANES), F32),
            vmem((2, NE, TILE, LANES), BF16),
            dma((4,)),
            dma((NE,)),
            dma((NE,)),
            dma((NE,)),
            dma((NE,)),
            dma((NC,)),
            dma((NC,)),
            dma((NE,)),
            dma((NE,)),
            dma,
            dma,
            dma((NE,)),
            dma((NE,)),
            dma((plan.nz,)),
            dma((plan.nz,)),
            dma((NE,)),
            dma((NE,)),
            dma,
            dma,
        ],
        compiler_params=pltpu.CompilerParams(
            collective_id=0, has_side_effects=True, vmem_limit_bytes=50 * 1024 * 1024
        ),
        cost_estimate=pl.CostEstimate(
            flops=6 * NE * 9 * width * hidden,
            bytes_accessed=6 * width * hidden,
            transcendentals=NE * 9 * hidden,
        ),
    )(
        tokens,
        routes.T,
        returns.reshape(1, count),
        router_weight.T,
        gate_weight,
        up_weight,
        down_weight,
        norm_gain.reshape(1, width),
        value_weight.reshape(1, width),
    )
    return values.reshape(count), grad.T


def solution(mesh):
    return jax.shard_map(
        functools.partial(on_device, mesh),
        mesh=mesh,
        in_specs=(
            P(("dp", "expert"), None),
            P(("dp", "expert"), None),
            P(("dp", "expert")),
            P(),
            P("expert", None, "tensor"),
            P("expert", None, "tensor"),
            P("expert", "tensor", None),
            P(),
            P(),
        ),
        out_specs=(P(("dp", "expert")), P()),
        check_vma=False,
    )
```

time: 2340 us -> 102 us (0.04)
  the two profiles are of different devices: /device:TPU:512 before, /device:TPU:1 now
where the time goes in v1:
time: 102 us
  Pallas kernels  95 us (93%)
  local copies, waits for them, and re-layouts  6.08 us (6%)
    pallas_call x1, Pallas kernels, on_device(): pl.pallas_call(functools.partial(expert_kernel, plan), out_shape=(jax.Sha...  95 us
    unnamed x10, local copies, waits for them, and re-layouts  4.65 us

profile of v1, /device:TPU:1, one launch (start us, length us, event | category | flops | bytes accessed | tf_op | source)
XLA Modules:
  0.0 101.8 jit_solution(14483028304286574952)
XLA Ops:
  0.6 0.7 reshape.17.gain_ref
  1.4 0.7 reshape.18.head_ref
  2.1 0.0 copy-start
  2.1 1.2 %copy-done = bf16[128,3584]{1,0:T(8,128)(2,1)S(1)} copy-done((bf16[128,3584]{1,0:T(8,128)(2,1)S(1)}, bf16[128,3584]{1,0:T(8,128)(2,1)}, u32[]{:S(2)}) %copy-start) | copy-done | bytes 917528
  3.3 0.0 copy-start.1
  3.3 0.9 copy-done.1
  4.2 0.0 copy-start.2
  4.2 0.7 copy-done.2
  4.9 0.0 copy-start.3
  4.9 0.7 copy-done.3
  5.5 95.0 %shard_map.104 = (f32[1,128]{1,0:T(1,128)S(1)}, bf16[32,3584]{1,0:T(8,128)(2,1)S(1)}) custom-call(bf16[128,3584]{1,0:T(8,128)(2,1)S(1)} %copy-done, s32[2,128]{1,0:T(2,128)S(1)} %bitcast.7, f32[1,128]{1,0:T(1,128)S(1)} %bitcast.8, bf16[32,3584]{1,0:T(8,128)(2,1)S(1)} %bitcast.6, bf16[1,3584,512]{2,1,0:T(8,128)(2,1)} %gate_hbm.1, ...), custom_call_target="tpu_custom_call" | custom-call | flops 3170893824 | bytes 11010048 | tf_op jit(solution)/shard_map/pallas_call | solution.py:482
  100.6 0.5 copy.13
  101.1 0.7 copy.14
Async XLA Ops:
  2.1 1.2 %copy-start = (bf16[128,3584]{1,0:T(8,128)(2,1)S(1)}, bf16[128,3584]{1,0:T(8,128)(2,1)}, u32[]{:S(2)}) copy-start(bf16[128,3584]{1,0:T(8,128)(2,1)} %tok_ref.1) | copy-start | bytes 2752516
  3.3 0.9 copy-start.1
  4.2 0.7 copy-start.2
  4.9 0.7 copy-start.3

commit v2 on v1

--- a/solution.py
+++ b/solution.py
@@ -21,8 +21,9 @@
         self.nz, self.groups = mesh.shape["dp"], mesh.shape["expert"]
         self.ny = 8 if self.groups >= 32 else 2
         self.nx = self.groups // self.ny
-        self.steps = ((0, 4), (3, 5), (2, 6), (1, 7)) if self.ny == 8 else ((0,), (1,))
+        self.steps = ((0, 4), (2, 6), (3, 5), (1, 7)) if self.ny == 8 else ((0,), (1,))
         self.chunks = len(self.steps)
+        self.home = [one[0] for one in self.steps].index(0)
         self.each = self.groups // self.chunks
         self.tokens, self.width, self.hidden = tokens, width, hidden
         self.half = width // 2
@@ -35,17 +36,24 @@
 
 def expert_kernel(
     plan,
+    tok_hbm,
+    routes_hbm,
+    returns_hbm,
+    router_hbm,
+    gate_hbm,
+    up_hbm,
+    down_hbm,
+    gain_hbm,
+    head_hbm,
+    values_ref,
+    grad_ref,
     tok_ref,
     routes_ref,
     returns_ref,
     router_ref,
-    gate_hbm,
-    up_hbm,
-    down_hbm,
     gain_ref,
     head_ref,
-    values_ref,
-    grad_ref,
+    gained_ref,
     wg,
     wu,
     wd,
@@ -58,6 +66,7 @@
     ret,
     back,
     qs,
+    answer,
     mix,
     nine,
     tmp9,
@@ -70,6 +79,8 @@
     zb,
     row9,
     agb,
+    values_out,
+    grad_out,
     w_sem,
     out_s,
     out_r,
@@ -97,6 +108,7 @@
     me = lax.axis_index("expert")
     c = lax.axis_index("tensor")
     other = 1 - c
+    own = plan.home * plan.each
     mx, my = lax.div(me, NY), lax.rem(me, NY)
 
     def hops(j, i):
@@ -117,16 +129,15 @@
             body(jnp.int32(j * CD) + i, i)
             return carry
 
-        lax.fori_loop(1 if j == 0 else 0, CD, run, 0)
-
-    loads = [
-        pltpu.make_async_copy(gate_hbm.at[0], wg, w_sem.at[0]),
-        pltpu.make_async_copy(up_hbm.at[0], wu, w_sem.at[1]),
-        pltpu.make_async_copy(down_hbm.at[0, :, pl.ds(0, H)], wd.at[0], w_sem.at[2]),
-        pltpu.make_async_copy(down_hbm.at[0, :, pl.ds(H, H)], wd.at[1], w_sem.at[3]),
-    ]
-    for load in loads:
-        load.start()
+        lax.fori_loop(1 if j == plan.home else 0, CD, run, 0)
+
+    def load(source, target, n):
+        return pltpu.make_async_copy(source, target, w_sem.at[n])
+
+    route_load = load(routes_hbm, routes_ref, 0)
+    route_load.start()
+    token_load = load(tok_hbm, tok_ref, 1)
+    token_load.start()
 
     barrier = pltpu.get_barrier_semaphore()
     for j in range(NC):
@@ -146,6 +157,21 @@
     lax.fori_loop(1, NZ, greet, 0)
     pl.semaphore_signal(barrier, inc=1, device_id=(z, me, other), device_id_type=MESH)
 
+    small_loads = [
+        load(router_hbm, router_ref, 2),
+        load(returns_hbm, returns_ref, 3),
+        load(gain_hbm, gain_ref, 4),
+        load(head_hbm, head_ref, 5),
+    ]
+    weight_loads = [
+        load(gate_hbm.at[0], wg, 6),
+        load(up_hbm.at[0], wu, 7),
+        load(down_hbm.at[0, :, pl.ds(0, H)], wd.at[0], 8),
+        load(down_hbm.at[0, :, pl.ds(H, H)], wd.at[1], 9),
+    ]
+    for one in small_loads + weight_loads:
+        one.start()
+
     def out_copy(j, d, i):
         return pltpu.make_async_remote_copy(
             out.at[d], arr.at[d], out_s.at[d], out_r.at[d], (z, ahead(j, i), c), MESH
@@ -172,21 +198,24 @@
             dlo.at[j], dli.at[d], dl_s.at[d], dl_r.at[d], (z, ahead(j, i), c), MESH
         )
 
+    def partner_of(l):
+        return jnp.where(l < MAIN, lax.shift_right_logical(l, 3), l - MAIN)
+
+    def slot_of(l):
+        slot = jnp.where(l < MAIN, jnp.bitwise_and(l, 7) + 1, EIGHT + 1)
+        return jnp.where(l < MAIN + CD, slot, -1).astype(F32)
+
+    def expert_of(l, j):
+        i = partner_of(l)
+        b = lax.shift_right_logical(i, NX.bit_length() - 1)
+        dy = jnp.full(l.shape, plan.steps[j][0], jnp.int32)
+        for n in range(1, len(plan.steps[j])):
+            dy = jnp.where(b == n, plan.steps[j][n], dy)
+        ex = jnp.bitwise_and(mx + jnp.bitwise_and(i, NX - 1), NX - 1)
+        return ex * NY + jnp.bitwise_and(my + dy, NY - 1)
+
     lane = lax.broadcasted_iota(jnp.int32, (1, LANES), 1)
-    lane_i = jnp.where(lane < MAIN, lax.shift_right_logical(lane, 3), lane - MAIN)
-    lane_slot = jnp.where(lane < MAIN, jnp.bitwise_and(lane, 7) + 1, EIGHT + 1)
-    lane_slot = jnp.where(lane < MAIN + CD, lane_slot, -1).astype(F32)
-    x_bits = NX.bit_length() - 1
-    lane_dx = jnp.bitwise_and(lane_i, NX - 1)
-    lane_b = lax.shift_right_logical(lane_i, x_bits)
-
-    def lane_expert(j):
-        dy = jnp.full((1, LANES), plan.steps[j][0], jnp.int32)
-        for b in range(1, len(plan.steps[j])):
-            dy = jnp.where(lane_b == b, plan.steps[j][b], dy)
-        ex = jnp.bitwise_and(mx + lane_dx, NX - 1)
-        ey = jnp.bitwise_and(my + dy, NY - 1)
-        return ex * NY + ey
+    lane_i, lane_slot = partner_of(lane), slot_of(lane)
 
     def pack(dst, j, rows):
         part = pl.ds(j * CD, CD)
@@ -209,34 +238,61 @@
         last = jnp.concatenate([last, jnp.zeros((XR - MAIN - CD, H), F32)], axis=0)
         put(MAIN, XR - MAIN, 0, H, last.astype(BF16))
 
-    expert_of_row = lax.broadcasted_iota(jnp.int32, (LANES, T), 0)
+    nine[...] = jnp.zeros_like(nine)
+    expert_row = lax.broadcasted_iota(jnp.int32, (NE, T), 0)
+    before = (
+        lax.broadcasted_iota(jnp.int32, (T, T), 0) < lax.broadcasted_iota(jnp.int32, (T, T), 1)
+    ).astype(BF16)
+    slot_row = lax.broadcasted_iota(jnp.int32, (XR, NE), 0)
+    expert_column = lax.broadcasted_iota(jnp.int32, (XR, NE), 1)
+    row_slot = slot_of(lax.broadcasted_iota(jnp.int32, (XR, T), 0))
+    spreads = [(expert_column == expert_of(slot_row, j)).astype(BF16) for j in range(NC)]
+    route_load.wait()
+    named = (expert_row == routes_ref[0:1, :]) | (expert_row == routes_ref[1:2, :])
+    named = named.astype(F32)
+    earlier = jnp.dot(named.astype(BF16), before, preferred_element_type=F32)
+    key = (named * (earlier + 1.0)).astype(BF16)
+    picks = []
+    for j in range(NC):
+        spread = jnp.dot(spreads[j], key, preferred_element_type=F32)
+        picks.append((spread == row_slot).astype(BF16))
+
+    columns = pl.ds(pl.multiple_of(c * H, LANES), H)
+    token_load.wait()
+    for j in range(NC):
+        pack(out, j, jnp.dot(picks[j], tok_ref[:, columns], preferred_element_type=F32))
+        if j == 0:
+            pl.semaphore_wait(barrier, NE - 1 + NZ - 1 + 1)
+        partners(j, lambda d, i, j=j: out_copy(j, d, i).start())
+        if j == plan.home:
+            arr[own] = out[own]
+            fwd_copy(own).start()
+
     marks = [
-        jnp.transpose((expert_of_row == routes_ref[k : k + 1, :]).astype(F32)) for k in range(2)
+        jnp.transpose(
+            (
+                lax.broadcasted_iota(jnp.int32, (LANES, T), 0) == routes_ref[k : k + 1, :]
+            ).astype(F32)
+        )
+        for k in range(2)
     ]
-    earlier = (
+    after = (
         lax.broadcasted_iota(jnp.int32, (T, T), 0) > lax.broadcasted_iota(jnp.int32, (T, T), 1)
     ).astype(BF16)
-    cum = jnp.dot(earlier, (marks[0] + marks[1]).astype(BF16), preferred_element_type=F32)
+    cum = jnp.dot(after, (marks[0] + marks[1]).astype(BF16), preferred_element_type=F32)
     key = jnp.concatenate([marks[0] * (cum + 1.0), marks[1] * (cum + 1.0)], axis=0).astype(BF16)
-    nine[...] = jnp.zeros_like(nine)
-
-    columns = pl.ds(pl.multiple_of(c * H, LANES), H)
-    for j in range(NC):
-        spread = (
-            lax.broadcasted_iota(jnp.int32, (LANES, LANES), 0) == lane_expert(j)
-        ).astype(BF16)
-        named = jnp.dot(key, spread, preferred_element_type=F32)
-        place = (named == lane_slot).astype(F32)
-        qs[j] = place.astype(BF16)
-        pick = jnp.transpose(place[0:T] + place[T : 2 * T])[0:XR].astype(BF16)
-        rows = jnp.dot(pick, tok_ref[:, columns], preferred_element_type=F32)
-        pack(out, j, rows)
-        if j == 0:
-            pl.semaphore_wait(barrier, NE - 1 + NZ - 1 + 1)
-            arr[0] = out[0]
-            fwd_copy(0).start()
-        partners(j, lambda d, i, j=j: out_copy(j, d, i).start())
-
+    for j in range(NC):
+        spread = (lax.broadcasted_iota(jnp.int32, (LANES, LANES), 0) == expert_of(lane, j)).astype(
+            BF16
+        )
+        spread = jnp.dot(key, spread, preferred_element_type=F32)
+        qs[j] = (spread == lane_slot).astype(F32).astype(BF16)
+
+    for one in small_loads:
+        one.wait()
+    for n in range(0, D, 2 * LANES):
+        gained = gain_ref[n : n + 2 * LANES] * head_ref[n : n + 2 * LANES].astype(F32)
+        gained_ref[:, n : n + 2 * LANES] = gained.reshape(1, 2 * LANES)
     logits = lax.dot_general(
         tok_ref[...], router_ref[...], (((1,), (1,)), ((), ())), preferred_element_type=F32
     )
@@ -245,8 +301,8 @@
         chosen = jnp.sum(marks[k][:, 0:NE] * scores, axis=1, keepdims=True)
         chosen_ref[k] = jnp.broadcast_to(chosen, (T, LANES))
 
-    for load in loads:
-        load.wait()
+    for one in weight_loads:
+        one.wait()
 
     for j in range(NC):
 
@@ -281,30 +337,31 @@
         px_copy(j).wait_recv()
         part = pl.ds(j * CD, CD)
         ret[part] = (ret[part].astype(F32) + pxi[part].astype(F32)).astype(BF16)
+        if j == plan.home:
+            back[own] = ret[own]
+        partners(j, lambda d, i, j=j: ret_copy(j, d, i).start())
+
+    for j in range(NC):
+        px_copy(j).wait_send()
+        partners(j, lambda d, i, j=j: out_copy(j, d, i).wait_send())
+
+    def left_chip(d, carry):
+        fwd_copy(d).wait_send()
+        return carry
+
+    lax.fori_loop(0, NE, left_chip, 0)
+
+    def put_answer(r, n, col, m, v):
+        answer[r : r + n, col : col + m] = v
+
+    for j in range(NC):
+        partners(j, lambda d, i, j=j: ret_copy(j, d, i).wait_recv())
+        unpack(back, j, put_answer)
+        term = jnp.dot(qs[j][:, 0:XR], answer[...], preferred_element_type=F32)
         if j == 0:
-            back[0] = ret[0]
-        partners(j, lambda d, i, j=j: ret_copy(j, d, i).start())
-
-    for j in range(NC):
-        partners(j, lambda d, i, j=j: ret_copy(j, d, i).wait_recv())
-
-        pieces = {}
-
-        def keep(r, n, col, m, v, pieces=pieces):
-            pieces[(r, col)] = v
-
-        unpack(back, j, keep)
-        low = qs[j][:, 0:MAIN]
-        high = qs[j][:, MAIN:XR]
-        for col in (0, Q4):
-            term = jnp.dot(low, pieces[(0, col)], preferred_element_type=F32)
-            term = term + jnp.dot(
-                high, pieces[(MAIN, 0)][:, col : col + Q4], preferred_element_type=F32
-            )
-            if j == 0:
-                mix[:, col : col + Q4] = term
-            else:
-                mix[:, col : col + Q4] += term
+            mix[...] = term
+        else:
+            mix[...] += term
 
     block = min(32, T)
     for b in range(T // block):
@@ -315,7 +372,7 @@
         acc = [jnp.zeros((block, LANES), F32) for _ in range(6)]
         for q in range(plan.pieces):
             at = pl.ds(pl.multiple_of(c * H + q * LANES, LANES), LANES)
-            gained = gain_ref[:, at] * head_ref[:, at].astype(F32)
+            gained = gained_ref[:, at]
             o0 = mix[low:high, q * LANES : (q + 1) * LANES]
             o1 = mix[T + low : T + high, q * LANES : (q + 1) * LANES]
             residual = tok_ref[low:high, at].astype(F32) + route_scale * (w0 * o0 + w1 * o1)
@@ -348,7 +405,6 @@
     rr, rg, ro0, ro1, go0, go1 = [sums[:, n : n + 1] for n in range(6)]
     inverse = lax.rsqrt(rr * (1.0 / D) + eps)
     values = rg * inverse
-    values_ref[...] = jnp.transpose(jnp.broadcast_to(values, (T, LANES)))[0:1, :]
     error = values - target
     pull = inverse * inverse * inverse * (error * rg * (1.0 / D))
     gw0 = route_scale * (inverse * error * go0 - pull * ro0)
@@ -360,9 +416,16 @@
 
     for j in range(NC):
         dlo[j] = jnp.sum(qs[j].astype(F32) * both, axis=0, keepdims=True)
-        if j == 0:
-            dli[0] = dlo[0]
+        if j == plan.home:
+            dli[own] = dlo[j]
         partners(j, lambda d, i, j=j: dl_copy(j, d, i).start())
+
+    values_out[...] = jnp.transpose(jnp.broadcast_to(values, (T, LANES)))[0:1, :]
+    values_store = pltpu.make_async_copy(values_out, values_ref, w_sem.at[10])
+    values_store.start()
+    sums_copy.wait_send()
+    for j in range(NC):
+        partners(j, lambda d, i, j=j: ret_copy(j, d, i).wait_send())
 
     grad = jnp.zeros((1, H), F32)
     for j in range(NC):
@@ -373,7 +436,10 @@
         line = jnp.broadcast_to(line, (TILE, LANES)).astype(BF16)[:, 0:XR]
         grad = grad + jnp.dot(line, xs[j, c], preferred_element_type=F32)[0:1]
 
-    zb[z] = grad
+    row9[...] = jnp.zeros_like(row9)
+    for q in range(plan.pieces):
+        row9[q : q + 1, :] = grad[:, q * LANES : (q + 1) * LANES]
+    zb[z] = row9[...].astype(BF16)
 
     def z_copy(dz):
         return pltpu.make_async_remote_copy(
@@ -395,15 +461,15 @@
         return carry
 
     lax.fori_loop(1, NZ, z_start, 0)
+    for j in range(NC):
+        partners(j, lambda d, i, j=j: dl_copy(j, d, i).wait_send())
+    values_store.wait()
     lax.fori_loop(1, NZ, z_wait, 0)
-    grad = zb[0]
+    grad = zb[0].astype(F32)
     for source in range(1, NZ):
-        grad = grad + zb[source]
-
-    row9[...] = jnp.zeros_like(row9)
-    for q in range(plan.pieces):
-        row9[q : q + 1, :] = grad[:, q * LANES : (q + 1) * LANES]
-    agb[c, me] = row9[...].astype(BF16)
+        grad = grad + zb[source].astype(F32)
+
+    agb[c, me] = grad.astype(BF16)
 
     def ag_copy(j, d, i):
         return pltpu.make_async_remote_copy(
@@ -418,6 +484,12 @@
 
     for j in range(NC):
         partners(j, lambda d, i, j=j: ag_copy(j, d, i).start())
+
+    def left_plane(dz, carry):
+        z_copy(dz).wait_send()
+        return carry
+
+    lax.fori_loop(1, NZ, left_plane, 0)
     for j in range(NC):
         partners(j, lambda d, i, j=j: ag_from(j, d, i).wait_recv())
     agx = pltpu.make_async_remote_copy(
@@ -425,38 +497,23 @@
     )
     agx.start()
 
-    for j in range(NC):
-        px_copy(j).wait_send()
-
-        def left(d, i, j=j):
-            out_copy(j, d, i).wait_send()
-            ret_copy(j, d, i).wait_send()
-            dl_copy(j, d, i).wait_send()
-            ag_copy(j, d, i).wait_send()
-
-        partners(j, left)
-
-    def left_chip(d, carry):
-        fwd_copy(d).wait_send()
-        return carry
-
-    def left_plane(dz, carry):
-        z_copy(dz).wait_send()
-        return carry
-
-    lax.fori_loop(0, NE, left_chip, 0)
-    lax.fori_loop(1, NZ, left_plane, 0)
-    sums_copy.wait_send()
-
-    def write(part):
+    def write(part, n):
         wide9[...] = agb[part].astype(F32).reshape(NE * TILE, LANES)
         for q in range(plan.pieces):
-            at = pl.ds(pl.multiple_of(part * H + q * LANES, LANES), LANES)
-            grad_ref[:, at] = wide9[pl.ds(q, NE, stride=TILE), :].astype(BF16)
-
-    write(c)
+            lanes = slice(q * LANES, (q + 1) * LANES)
+            grad_out[n, :, lanes] = wide9[pl.ds(q, NE, stride=TILE), :].astype(BF16)
+        at = pl.ds(pl.multiple_of(part * H, LANES), H)
+        store = pltpu.make_async_copy(grad_out.at[n], grad_ref.at[:, at], w_sem.at[11 + n])
+        store.start()
+        return store
+
+    first = write(c, 0)
+    for j in range(NC):
+        partners(j, lambda d, i, j=j: ag_copy(j, d, i).wait_send())
     agx.wait()
-    write(other)
+    second = write(other, 1)
+    first.wait()
+    second.wait()
 
 
 def on_device(
@@ -477,7 +534,6 @@
     NE, NC, H = plan.groups, plan.chunks, plan.half
     packed = (NE, TILE, plan.packed)
     vmem, dma = pltpu.VMEM, pltpu.SemaphoreType.DMA
-    in_vmem = pl.BlockSpec(memory_space=pltpu.VMEM)
     in_place = pl.BlockSpec(memory_space=pl.ANY)
     values, grad = pl.pallas_call(
         functools.partial(expert_kernel, plan),
@@ -485,9 +541,16 @@
             jax.ShapeDtypeStruct((1, count), F32),
             jax.ShapeDtypeStruct((NE, width), BF16),
         ),
-        in_specs=[in_vmem] * 4 + [in_place] * 3 + [in_vmem] * 2,
-        out_specs=(in_vmem, in_vmem),
+        in_specs=[in_place] * 9,
+        out_specs=(in_place, in_place),
         scratch_shapes=[
+            vmem((count, width), BF16),
+            vmem((2, count), jnp.int32),
+            vmem((1, count), F32),
+            vmem((NE, width), BF16),
+            vmem((width,), F32),
+            vmem((width,), BF16),
+            vmem((1, width), F32),
             vmem((width, hidden), BF16),
             vmem((width, hidden), BF16),
             vmem((2, hidden, H), BF16),
@@ -500,6 +563,7 @@
             vmem(packed, BF16),
             vmem(packed, BF16),
             vmem((NC, 2 * count, LANES), BF16),
+            vmem((plan.rows, H), BF16),
             vmem((2 * count, H), F32),
             vmem((plan.each * TILE, LANES), F32),
             vmem((plan.each * TILE, LANES), F32),
@@ -509,10 +573,12 @@
             vmem((count, LANES), F32),
             vmem((NC, 1, LANES), F32),
             vmem((NE, 1, LANES), F32),
-            vmem((plan.nz, 1, H), F32),
+            vmem((plan.nz, TILE, LANES), BF16),
             vmem((TILE, LANES), F32),
             vmem((2, NE, TILE, LANES), BF16),
-            dma((4,)),
+            vmem((1, count), F32),
+            vmem((2, NE, H), BF16),
+            dma((13,)),
             dma((NE,)),
             dma((NE,)),
             dma((NE,)),
@@ -533,7 +599,7 @@
             dma,
         ],
         compiler_params=pltpu.CompilerParams(
-            collective_id=0, has_side_effects=True, vmem_limit_bytes=50 * 1024 * 1024
+            collective_id=0, has_side_effects=True, vmem_limit_bytes=60 * 1024 * 1024
         ),
         cost_estimate=pl.CostEstimate(
             flops=6 * NE * 9 * width * hidden,
@@ -548,8 +614,8 @@
         gate_weight,
         up_weight,
         down_weight,
-        norm_gain.reshape(1, width),
-        value_weight.reshape(1, width),
+        norm_gain,
+        value_weight,
     )
     return values.reshape(count), grad.T
 

time: 102 us -> 98.8 us (0.969)
  local copies, waits for them, and re-layouts: 6.08 us -> 2.79 us
    unnamed x10 -> x2, local copies, waits for them, and re-layouts: 4.65 us -> 2.79 us
    reshape x2 -> x0, local copies, waits for them, and re-layouts: 1.44 us -> none  [the longest x1 0.73 us: on_device(): norm_gain.reshape(1, width)]
where the time goes in v2:
time: 98.8 us; the launch traced here: 98.7 us
  Pallas kernels  95.2 us (96%)
  local copies, waits for them, and re-layouts  2.79 us (3%)
    pallas_call x1, Pallas kernels, on_device(): pl.pallas_call(functools.partial(expert_kernel, plan), out_shape=(jax.Sha...  95.2 us
    unnamed x2, local copies, waits for them, and re-layouts  2.79 us

profile of v2, /device:TPU:1, one launch (start us, length us, event | category | flops | bytes accessed | tf_op | source)
XLA Modules:
  0.0 98.7 jit_solution(2609675512007473486)
XLA Ops:
  0.6 95.2 %shard_map.104 = (f32[1,128]{1,0:T(1,128)}, bf16[32,3584]{1,0:T(8,128)(2,1)}) custom-call(bf16[128,3584]{1,0:T(8,128)(2,1)} %tok_hbm.1, s32[2,128]{1,0:T(2,128)} %bitcast.7, f32[1,128]{1,0:T(1,128)} %bitcast.8, bf16[32,3584]{1,0:T(8,128)(2,1)} %bitcast.6, bf16[1,3584,512]{2,1,0:T(8,128)(2,1)} %gate_hbm.1, bf16[1,3584,512]{2,1,0:T(8,128)(2,1)} %up_hbm.1, ...), custom_call_target="tpu_custom_call" | custom-call | flops 3170893824 | bytes 11010048 | tf_op jit(solution)/shard_map/pallas_call | solution.py:538
  95.9 1.1 %copy.13 = f32[128]{0:T(128)} copy(f32[128]{0:T(128)} %bitcast.9) | data formatting | bytes 1024
  97.0 1.6 %copy.14 = bf16[3584,32]{0,1:T(8,128)(2,1)} copy(bf16[3584,32]{0,1:T(8,128)(2,1)} %bitcast.5) | data formatting | bytes 458752

commit v3 on v2

--- a/solution.py
+++ b/solution.py
@@ -79,8 +79,6 @@
     zb,
     row9,
     agb,
-    values_out,
-    grad_out,
     w_sem,
     out_s,
     out_r,
@@ -420,9 +418,7 @@
             dli[own] = dlo[j]
         partners(j, lambda d, i, j=j: dl_copy(j, d, i).start())
 
-    values_out[...] = jnp.transpose(jnp.broadcast_to(values, (T, LANES)))[0:1, :]
-    values_store = pltpu.make_async_copy(values_out, values_ref, w_sem.at[10])
-    values_store.start()
+    values_ref[...] = jnp.transpose(jnp.broadcast_to(values, (T, LANES)))[0:1, :]
     sums_copy.wait_send()
     for j in range(NC):
         partners(j, lambda d, i, j=j: ret_copy(j, d, i).wait_send())
@@ -463,7 +459,6 @@
     lax.fori_loop(1, NZ, z_start, 0)
     for j in range(NC):
         partners(j, lambda d, i, j=j: dl_copy(j, d, i).wait_send())
-    values_store.wait()
     lax.fori_loop(1, NZ, z_wait, 0)
     grad = zb[0].astype(F32)
     for source in range(1, NZ):
@@ -497,23 +492,17 @@
     )
     agx.start()
 
-    def write(part, n):
+    def write(part):
         wide9[...] = agb[part].astype(F32).reshape(NE * TILE, LANES)
         for q in range(plan.pieces):
-            lanes = slice(q * LANES, (q + 1) * LANES)
-            grad_out[n, :, lanes] = wide9[pl.ds(q, NE, stride=TILE), :].astype(BF16)
-        at = pl.ds(pl.multiple_of(part * H, LANES), H)
-        store = pltpu.make_async_copy(grad_out.at[n], grad_ref.at[:, at], w_sem.at[11 + n])
-        store.start()
-        return store
-
-    first = write(c, 0)
+            at = pl.ds(pl.multiple_of(part * H + q * LANES, LANES), LANES)
+            grad_ref[:, at] = wide9[pl.ds(q, NE, stride=TILE), :].astype(BF16)
+
+    write(c)
     for j in range(NC):
         partners(j, lambda d, i, j=j: ag_copy(j, d, i).wait_send())
     agx.wait()
-    second = write(other, 1)
-    first.wait()
-    second.wait()
+    write(other)
 
 
 def on_device(
@@ -542,7 +531,7 @@
             jax.ShapeDtypeStruct((NE, width), BF16),
         ),
         in_specs=[in_place] * 9,
-        out_specs=(in_place, in_place),
+        out_specs=(pl.BlockSpec(memory_space=pltpu.VMEM),) * 2,
         scratch_shapes=[
             vmem((count, width), BF16),
             vmem((2, count), jnp.int32),
@@ -576,9 +565,7 @@
             vmem((plan.nz, TILE, LANES), BF16),
             vmem((TILE, LANES), F32),
             vmem((2, NE, TILE, LANES), BF16),
-            vmem((1, count), F32),
-            vmem((2, NE, H), BF16),
-            dma((13,)),
+            dma((10,)),
             dma((NE,)),
             dma((NE,)),
             dma((NE,)),
@@ -599,7 +586,7 @@
             dma,
         ],
         compiler_params=pltpu.CompilerParams(
-            collective_id=0, has_side_effects=True, vmem_limit_bytes=60 * 1024 * 1024
+            collective_id=0, has_side_effects=True, vmem_limit_bytes=48 * 1024 * 1024
         ),
         cost_estimate=pl.CostEstimate(
             flops=6 * NE * 9 * width * hidden,
@@ -607,15 +594,20 @@
             transcendentals=NE * 9 * hidden,
         ),
     )(
-        tokens,
-        routes.T,
-        returns.reshape(1, count),
-        router_weight.T,
-        gate_weight,
-        up_weight,
-        down_weight,
-        norm_gain,
-        value_weight,
+        *(
+            pltpu.with_memory_space_constraint(operand, pltpu.HBM)
+            for operand in (
+                tokens,
+                routes.T,
+                returns.reshape(1, count),
+                router_weight.T,
+                gate_weight,
+                up_weight,
+                down_weight,
+                norm_gain,
+                value_weight,
+            )
+        )
     )
     return values.reshape(count), grad.T
 

time: 98.8 us -> 96.5 us (0.977)
  local copies, waits for them, and re-layouts: 2.79 us -> 1.2 us
    unnamed x2, local copies, waits for them, and re-layouts: 2.79 us -> 1.2 us
where the time goes in v3:
time: 96.5 us; the launch traced here: 96.4 us
  Pallas kernels  94.5 us (98%)
  local copies, waits for them, and re-layouts  1.2 us (1%)
    pallas_call x1, Pallas kernels, on_device(): pl.pallas_call(functools.partial(expert_kernel, plan), out_shape=(jax.Sha...  94.5 us

profile of v3, /device:TPU:1, one launch (start us, length us, event | category | flops | bytes accessed | tf_op | source)
XLA Modules:
  0.0 96.4 jit_solution(5641380013727512017)
XLA Ops:
  0.6 94.5 %shard_map.104 = (f32[1,128]{1,0:T(1,128)S(1)}, bf16[32,3584]{1,0:T(8,128)(2,1)S(1)}) custom-call(bf16[128,3584]{1,0:T(8,128)(2,1)} %tok_hbm.1, s32[2,128]{1,0:T(2,128)} %bitcast.8, f32[1,128]{1,0:T(1,128)} %bitcast.9, bf16[32,3584]{1,0:T(8,128)(2,1)} %bitcast.7, bf16[1,3584,512]{2,1,0:T(8,128)(2,1)} %gate_hbm.1, bf16[1,3584,512]{2,1,0:T(8,128)(2,1)} %up_hbm.1, ...), custom_call_target="tpu_custom_call" | custom-call | flops 3170893824 | bytes 11010048 | tf_op jit(solution)/shard_map/pallas_call | solution.py:527
  95.2 0.5 copy.13
  95.7 0.7 copy.14

commit v4 on v3

--- a/solution.py
+++ b/solution.py
@@ -23,6 +23,7 @@
         self.nx = self.groups // self.ny
         self.steps = ((0, 4), (2, 6), (3, 5), (1, 7)) if self.ny == 8 else ((0,), (1,))
         self.chunks = len(self.steps)
+        self.joined = ((0, 1, 2), (3,)) if self.chunks == 4 else ((0, 1),)
         self.home = [one[0] for one in self.steps].index(0)
         self.each = self.groups // self.chunks
         self.tokens, self.width, self.hidden = tokens, width, hidden
@@ -66,6 +67,7 @@
     ret,
     back,
     qs,
+    joined,
     answer,
     mix,
     nine,
@@ -279,12 +281,18 @@
     ).astype(BF16)
     cum = jnp.dot(after, (marks[0] + marks[1]).astype(BF16), preferred_element_type=F32)
     key = jnp.concatenate([marks[0] * (cum + 1.0), marks[1] * (cum + 1.0)], axis=0).astype(BF16)
+    places = []
     for j in range(NC):
         spread = (lax.broadcasted_iota(jnp.int32, (LANES, LANES), 0) == expert_of(lane, j)).astype(
             BF16
         )
         spread = jnp.dot(key, spread, preferred_element_type=F32)
-        qs[j] = (spread == lane_slot).astype(F32).astype(BF16)
+        place = (spread == lane_slot).astype(F32)
+        qs[j] = place.astype(BF16)
+        places.append(place[:, 0:XR])
+    for n, steps in enumerate(plan.joined):
+        place = jnp.concatenate([places[j] for j in steps], axis=1)
+        joined[n, :, 0 : len(steps) * XR] = place.astype(BF16)
 
     for one in small_loads:
         one.wait()
@@ -349,14 +357,17 @@
 
     lax.fori_loop(0, NE, left_chip, 0)
 
-    def put_answer(r, n, col, m, v):
-        answer[r : r + n, col : col + m] = v
-
-    for j in range(NC):
-        partners(j, lambda d, i, j=j: ret_copy(j, d, i).wait_recv())
-        unpack(back, j, put_answer)
-        term = jnp.dot(qs[j][:, 0:XR], answer[...], preferred_element_type=F32)
-        if j == 0:
+    for n, steps in enumerate(plan.joined):
+        for k, j in enumerate(steps):
+
+            def put_answer(r, rows, col, m, v, first=k * XR):
+                answer[first + r : first + r + rows, col : col + m] = v
+
+            partners(j, lambda d, i, j=j: ret_copy(j, d, i).wait_recv())
+            unpack(back, j, put_answer)
+        deep = len(steps) * XR
+        term = jnp.dot(joined[n, :, 0:deep], answer[0:deep], preferred_element_type=F32)
+        if n == 0:
             mix[...] = term
         else:
             mix[...] += term
@@ -437,9 +448,10 @@
         row9[q : q + 1, :] = grad[:, q * LANES : (q + 1) * LANES]
     zb[z] = row9[...].astype(BF16)
 
-    def z_copy(dz):
-        return pltpu.make_async_remote_copy(
-            zb.at[z], zb.at[z], z_s.at[dz], z_r.at[z], (lax.rem(z + dz, NZ), me, c), MESH
+    def z_copy(n):
+        dz = lax.rem(n + NZ // 2 - 1, NZ - 1) + 1
+        return pltpu.make_async_remote_copy(
+            zb.at[z], zb.at[z], z_s.at[n], z_r.at[z], (lax.rem(z + dz, NZ), me, c), MESH
         )
 
     def z_from(dz):
@@ -552,7 +564,8 @@
             vmem(packed, BF16),
             vmem(packed, BF16),
             vmem((NC, 2 * count, LANES), BF16),
-            vmem((plan.rows, H), BF16),
+            vmem((len(plan.joined), 2 * count, 2 * LANES), BF16),
+            vmem((max(map(len, plan.joined)) * plan.rows, H), BF16),
             vmem((2 * count, H), F32),
             vmem((plan.each * TILE, LANES), F32),
             vmem((plan.each * TILE, LANES), F32),

time: 96.5 us -> 96.7 us (level)
  no operation moved by 1% of the time
where the time goes in v4:
time: 96.7 us; the launch traced here: 96.5 us
  Pallas kernels  94.7 us (98%)
  local copies, waits for them, and re-layouts  1.2 us (1%)
    pallas_call x1, Pallas kernels, on_device(): pl.pallas_call(functools.partial(expert_kernel, plan), out_shape=(jax.Sha...  94.7 us

profile of v4, /device:TPU:1, one launch (start us, length us, event | category | flops | bytes accessed | tf_op | source)
XLA Modules:
  0.0 96.5 jit_solution(16118169928380904821)
XLA Ops:
  0.6 94.7 %shard_map.104 = (f32[1,128]{1,0:T(1,128)S(1)}, bf16[32,3584]{1,0:T(8,128)(2,1)S(1)}) custom-call(bf16[128,3584]{1,0:T(8,128)(2,1)} %tok_hbm.1, s32[2,128]{1,0:T(2,128)} %bitcast.8, f32[1,128]{1,0:T(1,128)} %bitcast.9, bf16[32,3584]{1,0:T(8,128)(2,1)} %bitcast.7, bf16[1,3584,512]{2,1,0:T(8,128)(2,1)} %gate_hbm.1, bf16[1,3584,512]{2,1,0:T(8,128)(2,1)} %up_hbm.1, ...), custom_call_target="tpu_custom_call" | custom-call | flops 3170893824 | bytes 11010048 | tf_op jit(solution)/shard_map/pallas_call | solution.py:539
  95.3 0.5 copy.13
  95.8 0.7 copy.14

commit v5 on v4

--- a/solution.py
+++ b/solution.py
@@ -134,12 +134,15 @@
     def load(source, target, n):
         return pltpu.make_async_copy(source, target, w_sem.at[n])
 
-    route_load = load(routes_hbm, routes_ref, 0)
-    route_load.start()
-    token_load = load(tok_hbm, tok_ref, 1)
-    token_load.start()
-
     barrier = pltpu.get_barrier_semaphore()
+    def greet(dz, carry):
+        pl.semaphore_signal(
+            barrier, inc=1, device_id=(lax.rem(z + dz, NZ), me, c), device_id_type=MESH
+        )
+        return carry
+
+    lax.fori_loop(1, NZ, greet, 0)
+
     for j in range(NC):
         partners(
             j,
@@ -147,15 +150,12 @@
                 barrier, inc=1, device_id=(z, ahead(j, i), c), device_id_type=MESH
             ),
         )
-
-    def greet(dz, carry):
-        pl.semaphore_signal(
-            barrier, inc=1, device_id=(lax.rem(z + dz, NZ), me, c), device_id_type=MESH
-        )
-        return carry
-
-    lax.fori_loop(1, NZ, greet, 0)
     pl.semaphore_signal(barrier, inc=1, device_id=(z, me, other), device_id_type=MESH)
+
+    route_load = load(routes_hbm, routes_ref, 0)
+    route_load.start()
+    token_load = load(tok_hbm, tok_ref, 1)
+    token_load.start()
 
     small_loads = [
         load(router_hbm, router_ref, 2),

time: 96.7 us -> 95.8 us (level)
  no operation moved by 1% of the time
where the time goes in v5:
time: 95.8 us; the launch traced here: 95.7 us
  Pallas kernels  93.9 us (98%)
  local copies, waits for them, and re-layouts  1.2 us (1%)
    pallas_call x1, Pallas kernels, on_device(): pl.pallas_call(functools.partial(expert_kernel, plan), out_shape=(jax.Sha...  93.9 us

profile of v5, /device:TPU:1, one launch (start us, length us, event | category | flops | bytes accessed | tf_op | source)
XLA Modules:
  0.0 95.7 jit_solution(17777654918757006976)
XLA Ops:
  0.6 93.9 %shard_map.104 = (f32[1,128]{1,0:T(1,128)S(1)}, bf16[32,3584]{1,0:T(8,128)(2,1)S(1)}) custom-call(bf16[128,3584]{1,0:T(8,128)(2,1)} %tok_hbm.1, s32[2,128]{1,0:T(2,128)} %bitcast.8, f32[1,128]{1,0:T(1,128)} %bitcast.9, bf16[32,3584]{1,0:T(8,128)(2,1)} %bitcast.7, bf16[1,3584,512]{2,1,0:T(8,128)(2,1)} %gate_hbm.1, bf16[1,3584,512]{2,1,0:T(8,128)(2,1)} %up_hbm.1, ...), custom_call_target="tpu_custom_call" | custom-call | flops 3170893824 | bytes 11010048 | tf_op jit(solution)/shard_map/pallas_call | solution.py:539
  94.5 0.5 copy.13
  95.0 0.7 copy.14
